TPU v7x, 32 devices: a whole 2x2x4 slice. The times are simulated.
32 devices in a mesh: dp: 4 (over z), gy: 4 (over y, core), gz: 2 (over x).
Axes of the slice: x: 2, y: 2, z: 4, core: 2. Of those that a mesh axis runs over, the one named last changes fastest.
Arguments:
- volume: bfloat16 [4, 4, 16, 32, 128], P('dp', None, 'gy', 'gz'), may hold values from -6 to 6
- pooled_first: bfloat16 [4, 16, 8, 16, 64], P('dp', None, 'gy', 'gz'), may hold values from -6 to 6
- where_first: int32 [4, 16, 8, 16, 64], P('dp', None, 'gy', 'gz'), may hold values from 0 to 7
- pooled_second: bfloat16 [4, 32, 4, 8, 32], P('dp', None, 'gy', 'gz'), may hold values from -6 to 6
- where_second: int32 [4, 32, 4, 8, 32], P('dp', None, 'gy', 'gz'), may hold values from 0 to 7
- upstream: bfloat16 [4, 32, 4, 8, 32], P('dp', None, 'gy', 'gz'), may hold values from -6 to 6
- kernel_first: bfloat16 [16, 4, 3, 3, 3], replicated, may hold values from -0.625 to 0.625
- kernel_second: bfloat16 [32, 16, 3, 3, 3], replicated, may hold values from -0.3125 to 0.3125
Outputs:
- grad_volume: bfloat16 [4, 4, 16, 32, 128], P('dp', None, 'gy', 'gz')
- grad_kernel_first: float32 [1728], P('dp')
- grad_kernel_second: float32 [13824], P('dp')
All inputs are finite; a program needn't handle non-finite values.
Results may differ from a plain program's by a relative error of at most 0.005.
Values may be sent and summed in bfloat16 or wider, within the bound.
No kernel may reach another device: no remote copies, remote signals or barrier semaphores. Data moves between devices by JAX's collectives and lax.ppermute only.
A program may use at most 64 MiB of HBM per device.

v0:
```python
import functools
import math

import jax
import jax.numpy as jnp
from jax import lax
from jax.experimental import pallas as pl
from jax.experimental.pallas import tpu as pltpu
from jax.sharding import PartitionSpec as P

leak_rate = 0.3
lanes = 128
f32, bf16 = jnp.float32, jnp.bfloat16


def dot(a, b):
    return lax.dot_general(a, b, (((1,), (0,)), ((), ())), preferred_element_type=f32)


def dot_nt(a, b):
    return lax.dot_general(a, b, (((1,), (1,)), ((), ())), preferred_element_type=f32)


def spread_matrix(first_row, count):
    row = lax.broadcasted_iota(jnp.int32, (lanes, lanes), 0)
    lane = lax.broadcasted_iota(jnp.int32, (lanes, lanes), 1)
    hit = (lane >> 1) + first_row == row
    return jnp.where(hit & (lane < 2 * count), 1.0, 0.0).astype(bf16)


def order_matrix(ins, shape, tap):
    row = lax.broadcasted_iota(jnp.int32, shape, 0)
    column = lax.broadcasted_iota(jnp.int32, shape, 1)
    hit = column == (row % ins) * 27 + 3 * tap + row // ins
    return jnp.where(hit & (row < 3 * ins), 1.0, 0.0).astype(bf16)


def rows_of(count):
    return -(-count // lanes)


def flat_rows(values, length, keep, shards_dp):
    starts = [length * k % lanes for k in range(keep)]
    width = rows_of(max(starts) + length) * lanes
    if values.shape[1] < width:
        blank = jnp.zeros((values.shape[0], width - values.shape[1]), f32)
        values = jnp.concatenate([values, blank], 1)
    turned = {n: pltpu.roll(values, n, 1) if n else values for n in sorted(set(starts))}
    shards = []
    for d in range(shards_dp):
        rows = [None] * rows_of(length * keep)
        for k, start in enumerate(starts):
            for t in range(rows_of(start + length)):
                at = length * k // lanes + t
                piece = turned[start][d * keep + k : d * keep + k + 1, t * lanes : (t + 1) * lanes]
                rows[at] = piece if rows[at] is None else rows[at] + piece
        shards.append(rows)
    return shards


def prepare_kernel(kinds, odd_ref, *refs):
    count = 2 + kinds
    inputs, outputs, refs = refs[:5], refs[5 : 5 + count], refs[5 + count :]
    copies, arrived = refs[:5], refs[5]
    moves = [
        pltpu.make_async_copy(source, target, arrived.at[n])
        for n, (source, target) in enumerate(zip(inputs, copies))
    ]
    for move in moves:
        move.start()
    for move in moves:
        move.wait()
    prepare(odd_ref, *copies, *outputs[:2], outputs[2:])


def prepare(
    odd_ref,
    upstream_ref,
    pooled_second_ref,
    where_second_ref,
    pooled_first_ref,
    where_first_ref,
    even_ref,
    odd_plane_ref,
    rim_refs,
):
    c1, ys, zs, xs = pooled_first_ref.shape[1:]
    zq = zs // 2
    odd_z, odd_y = odd_ref[0] > 0, odd_ref[1] > 0
    slope = jnp.where(pooled_second_ref[0, :, 0].astype(f32) > 0, 1.0, leak_rate)
    value = upstream_ref[0, :, 0].astype(f32) * slope
    place = (where_second_ref[0, :, 0] + 1).astype(f32)
    quarter = [jnp.transpose(part, (1, 0, 2)) for part in (value, place)]
    for n, part in enumerate(quarter):
        row = jnp.concatenate([part[z] for z in range(zq)], 1).astype(bf16)
        even_ref[zq + n] = row
        odd_plane_ref[zq + n] = row
    fill = jnp.zeros((2 * c1, lanes - xs - xs // 2), f32)
    packed = []
    for y in range(ys):
        pooled = jnp.transpose(pooled_first_ref[0, :, y].astype(f32), (1, 0, 2))
        places = jnp.transpose((where_first_ref[0, :, y] + 1).astype(f32), (1, 0, 2))
        rows = [jnp.concatenate([pooled[z], places[z]], 0) for z in range(zs)]
        packed.append(
            [jnp.concatenate([rows[2 * n], rows[2 * n + 1]], 1).astype(bf16) for n in range(zq)]
        )
        low = jnp.concatenate([rows[0], quarter[y][0], fill], 1)
        high = jnp.concatenate([rows[-1], quarter[y][-1], fill], 1)
        for n, ref in enumerate(rim_refs):
            ref[y] = jnp.where(odd_z == (n == 0), low, high).astype(bf16)
    for n in range(zq):
        even_ref[n] = jnp.where(odd_y, packed[0][n], packed[-1][n])
        odd_plane_ref[n] = jnp.where(odd_y, packed[-1][n], packed[0][n])


def sides_of(refs, odd):
    even = refs[0][...]
    other = refs[1][...] if len(refs) > 1 else jnp.zeros_like(even)
    return jnp.where(odd, even, other), jnp.where(odd, other, even)


def unpooled(values, places, parity):
    return [
        [
            jnp.where(places == parity + (4 * dy + 2 * dz), values, 0.0).astype(bf16)
            for dz in range(2)
        ]
        for dy in range(2)
    ]


def lane_parity():
    lane = lax.broadcasted_iota(jnp.int32, (1, lanes), 1)
    return (lane & 1).astype(f32) + 1.0


def spread_quarter(values, places, xs, c2, zq):
    wide = jnp.concatenate([spread_matrix(z * xs // 2, xs // 2) for z in range(zq)], 1)
    found = dot(jnp.concatenate([values, places], 0), wide)
    return [
        (found[:c2, z * lanes : (z + 1) * lanes], found[c2:, z * lanes : (z + 1) * lanes])
        for z in range(zq)
    ]


def spread_places(plane, ends, xs, c1, zq):
    wide = jnp.concatenate([spread_matrix(0, xs), spread_matrix(xs, xs)], 1)
    rows = [plane[n][c1:] for n in range(zq)] + [end[c1:] for end in ends]
    found = dot(jnp.concatenate(rows, 0), wide)
    inner = [
        found[n * c1 : (n + 1) * c1, m * lanes : (m + 1) * lanes]
        for n in range(zq)
        for m in range(2)
    ]
    outer = [found[n * c1 : (n + 1) * c1, :lanes] for n in range(zq, zq + len(ends))]
    return outer[:1] + inner + outer[1:]


def side_kernel(
    sizes,
    odd_ref,
    own_refs,
    rim_refs,
    plane_refs,
    volume_ref,
    first_ref,
    second_ref,
    up_ref,
    places_ref,
    side_up_ref,
    side_places_ref,
    cells_ref,
    first_out_ref,
    second_out_ref,
    first_order_ref,
    second_order_ref,
):
    ys, zs, xs, c1, c2 = sizes
    zlow, zhigh = sides_of(rim_refs, odd_ref[0] > 0)
    own = sides_of(own_refs, odd_ref[1] > 0)
    parity = lane_parity()
    zq = zs // 2
    rows = spread_quarter(own[0][zq], own[0][zq + 1], xs, c2, zq)
    rims = jnp.concatenate([zlow[0], zlow[1], zhigh[0], zhigh[1]], 0)
    rims = dot(rims, spread_matrix(xs, xs // 2))
    rims = [rims[n * c2 : (n + 1) * c2] for n in range(4)]
    rows = [(rims[0], rims[1])] + rows + [(rims[2], rims[3])]
    for n, (value, place) in enumerate(rows):
        cells = unpooled(value, place, parity)
        for dy in range(2):
            for dz in range(2):
                up_ref[dy, 2 * n + dz] = cells[dy][dz]
    for y in range(ys):
        for n, row in enumerate(spread_places(own[y], (zlow[y], zhigh[y]), xs, c1, zq)):
            places_ref[y, n] = row.astype(bf16)
    for side, plane in enumerate(sides_of(plane_refs, odd_ref[1] > 0)):
        for n, (value, place) in enumerate(spread_quarter(plane[zq], plane[zq + 1], xs, c2, zq)):
            cells = unpooled(value, place, parity)
            for dy in range(2):
                for dz in range(2):
                    side_up_ref[side, dy, 2 * n + dz] = cells[dy][dz]
        for n, row in enumerate(spread_places(plane, (), xs, c1, zq)):
            side_places_ref[side, n] = row.astype(bf16)

    lane = lax.broadcasted_iota(jnp.int32, (1, 1, lanes), 2)
    c0, _, zf = volume_ref.shape[1:4]
    for y in range(2 * ys):
        cell = volume_ref[0, :, y].astype(f32)
        moved = [
            jnp.where(lane > 0, pltpu.roll(cell, 1, 2), 0.0),
            cell,
            jnp.where(lane < lanes - 1, pltpu.roll(cell, lanes - 1, 2), 0.0),
            jnp.zeros_like(cell),
        ]
        turned = jnp.transpose(jnp.concatenate(moved, 0), (1, 0, 2))
        for z in range(zf):
            cells_ref[y, :, z * lanes : (z + 1) * lanes] = turned[z].astype(bf16)

    wide = []
    for tap in range(9):
        parts = []
        for tx in range(3):
            parts += [first_ref[3 * tap + tx].astype(f32), jnp.zeros((8 - c0, c1), f32)]
        wide.append(jnp.concatenate(parts, 0))
    first_out_ref[...] = jnp.concatenate(wide, 1).astype(bf16)
    wide = [
        jnp.concatenate([second_ref[3 * tap + tx].astype(f32) for tx in range(3)], 0)
        for tap in range(9)
    ]
    second_out_ref[...] = jnp.concatenate(wide, 1).astype(bf16)
    for tap in range(9):
        first_order_ref[tap] = order_matrix(c0, first_order_ref.shape[1:], tap)
        second_order_ref[tap] = order_matrix(c1, second_order_ref.shape[1:], tap)


def main_kernel(
    sizes,
    odd_ref,
    own_refs,
    rim_refs,
    plane_refs,
    row_refs,
    own_up_ref,
    own_places_ref,
    side_up_ref,
    side_places_ref,
    volume_ref,
    first_ref,
    second_ref,
    first_order_ref,
    second_order_ref,
    grad_ref,
    sums_ref,
    up_ref,
    down_ref,
    cells_ref,
    leaving_ref,
    sent,
):
    ys, zs, xs, c1, c2 = sizes
    zq = zs // 2
    odd_z, odd_y = odd_ref[0] > 0, odd_ref[1] > 0
    zlow, zhigh = sides_of(rim_refs, odd_z)
    own = sides_of(own_refs, odd_y)
    planes = sides_of(plane_refs, odd_y)
    even_rims, other_rims = [
        sides_of([ref[n] for n in range(len(rim_refs))], odd_z) for ref in row_refs
    ]
    plane_rims = [
        [jnp.where(odd_y, even_rims[n], other_rims[n]) for n in range(2)],
        [jnp.where(odd_y, other_rims[n], even_rims[n]) for n in range(2)],
    ]
    parity = lane_parity()
    lane = lax.broadcasted_iota(jnp.int32, (1, lanes), 1)

    near, far = spread_matrix(xs, xs // 2), spread_matrix(xs + xs // 2, xs // 2)
    for side in range(2):
        ends = jnp.concatenate(plane_rims[side], 0)
        values, places = dot(ends, near), dot(ends, far)
        for n in range(2):
            at = slice(n * c2, (n + 1) * c2)
            cells = unpooled(values[at], places[at], parity)
            for dy in range(2):
                for dz in range(2):
                    up_ref[side, dy, 2 * n + dz] = cells[dy][dz]

    def up_row(y, z):
        if 0 <= y < ys:
            return own_up_ref[y, z + 2]
        side, dy = (0, y + 2) if y < 0 else (1, y - ys)
        if 0 <= z < zs:
            return side_up_ref[side, dy, z]
        return up_ref[side, dy, z + 2 if z < 0 else z + 2 - zs]

    def pooled_row(y, z):
        side = None if 0 <= y < ys else int(y >= ys)
        if 0 <= z < zs:
            plane = own[y] if side is None else planes[side]
            row = plane[z // 2][:c1].astype(f32)
            return pltpu.roll(row, lanes - xs, 1) if z % 2 else row
        at = int(z >= 0)
        rim = (zlow, zhigh)[at][y] if side is None else plane_rims[side][at]
        return rim[:c1].astype(f32)

    rim_places = jnp.concatenate([end[c1:] for rims in plane_rims for end in rims], 0)
    rim_places = dot(rim_places, spread_matrix(0, xs))

    def place_row(y, n):
        if 0 <= y < ys:
            return own_places_ref[y, n].astype(f32)
        side = int(y >= ys)
        if 0 < n <= zs:
            return side_places_ref[side, n - 1].astype(f32)
        at = 2 * side + int(n > 0)
        return rim_places[at * c1 : (at + 1) * c1]

    spread = spread_matrix(0, xs)
    weights = second_ref[...]
    second_sum = None
    for y in range(-1, ys + 1):
        zr = range(-1, zs + 1)
        around = jnp.concatenate(
            [
                jnp.concatenate([up_row(y + 1 - ty, z + 1 - tz) for z in zr], 1)
                for ty in range(3)
                for tz in range(3)
            ],
            0,
        )
        terms = dot(weights, around)
        rows = [pooled_row(y, z) for z in zr]
        grads = []
        for n, pooled in enumerate(rows):
            at = slice(n * lanes, (n + 1) * lanes)
            total = (
                pltpu.roll(terms[:c1, at], lanes - 1, 1)
                + terms[c1 : 2 * c1, at]
                + pltpu.roll(terms[2 * c1 :, at], 1, 1)
            )
            grads.append((total * jnp.where(pooled > 0, 1.0, leak_rate)).astype(bf16))
        values = dot(jnp.concatenate(grads, 0), spread)
        for n, z in enumerate(zr):
            cells = unpooled(values[n * c1 : (n + 1) * c1], place_row(y, n), parity)
            for dy in range(2):
                for dz in range(2):
                    down_ref[2 * y + 2 + dy, 2 * z + 2 + dz] = cells[dy][dz]
        if 0 <= y < ys:
            inputs = []
            for pooled in rows[1:-1]:
                act = jnp.where(pooled > 0, pooled, leak_rate * pooled)
                act = jnp.where(lane < xs, act, 0.0).astype(bf16).astype(f32)
                inputs.append(
                    jnp.concatenate(
                        [pltpu.roll(act, 1, 1), act, pltpu.roll(act, lanes - 1, 1)], 0
                    ).astype(bf16)
                )
            term = dot_nt(jnp.concatenate(inputs, 1), around[:, lanes:-lanes])
            second_sum = term if second_sum is None else second_sum + term

    weights = first_ref[...]
    first_sum = None
    leaving = []
    c0 = grad_ref.shape[0]
    for y in range(2 * ys):
        zr = range(2 * zs)
        around = jnp.concatenate(
            [
                jnp.concatenate([down_ref[y + 3 - ty, z + 3 - tz] for z in zr], 1)
                for ty in range(3)
                for tz in range(3)
            ],
            0,
        )
        terms = dot(weights, around)
        for z in zr:
            at = slice(z * lanes, (z + 1) * lanes)
            left = jnp.where(lane < lanes - 1, pltpu.roll(terms[:8, at], lanes - 1, 1), 0.0)
            right = jnp.where(lane > 0, pltpu.roll(terms[16:, at], 1, 1), 0.0)
            total = left + terms[8:16, at] + right
            for i in range(c0):
                cells_ref[i, y, z : z + 1, :] = total[i : i + 1]
        leaving_ref[:, y] = cells_ref[:, y].astype(bf16)
        leaving.append(pltpu.make_async_copy(leaving_ref.at[:, y], grad_ref.at[:, y], sent.at[y]))
        leaving[y].start()
        term = dot_nt(volume_ref[y], around)
        first_sum = term if first_sum is None else first_sum + term

    first_sum, second_sum = first_sum.T, second_sum.T
    first, second = 0.0, 0.0
    for tap in range(9):
        first += dot(first_sum[tap * c1 : (tap + 1) * c1].astype(bf16), first_order_ref[tap])
        second += dot(second_sum[tap * c2 : (tap + 1) * c2].astype(bf16), second_order_ref[tap])

    shards_dp, count = sums_ref.shape[:2]
    seconds = flat_rows(second, 27 * c1, c2 // shards_dp, shards_dp)
    firsts = flat_rows(first, 27 * c0, c1 // shards_dp, shards_dp)
    for d in range(shards_dp):
        rows = seconds[d] + firsts[d]
        if len(rows) < count:
            rows = rows + [jnp.zeros((count - len(rows), lanes), f32)]
        sums_ref[d] = jnp.concatenate(rows, 0).astype(bf16)
    for move in leaving:
        move.wait()


def shards(
    volume,
    pooled_first,
    where_first,
    pooled_second,
    where_second,
    upstream,
    kernel_first,
    kernel_second,
):
    dp, gy, gz = (lax.axis_size(a) for a in ("dp", "gy", "gz"))
    c0, c1, c2 = volume.shape[1], pooled_first.shape[1], pooled_second.shape[1]
    ys, zs, xs = pooled_first.shape[2:]

    odd_z, odd_y = lax.axis_index("gz") % 2 == 1, lax.axis_index("gy") % 2 == 1
    odd = jnp.stack([odd_z, odd_y]).astype(jnp.int32)
    smem = pl.BlockSpec(memory_space=pltpu.SMEM)
    vmem = pl.BlockSpec(memory_space=pltpu.VMEM)
    params = pltpu.CompilerParams(vmem_limit_bytes=48 * 1024 * 1024)

    def like(*shape):
        return jax.ShapeDtypeStruct(shape, bf16)

    def pairs_of(axis, begin):
        count = lax.axis_size(axis)
        pairs = [(i, i + 1) for i in range(begin, count - 1, 2)]
        return pairs + [(b, a) for a, b in pairs]

    kinds = 2 if gz > 2 else 1
    raw = (upstream, pooled_second, where_second, pooled_first, where_first)
    plane = like(zs // 2 + 2, 2 * c1, lanes)
    prepared = (plane, plane) + (like(2, 2 * c1, lanes),) * kinds
    even, other, *rims = pl.pallas_call(
        functools.partial(prepare_kernel, kinds),
        out_shape=tuple(pltpu.VMEM(a.shape, a.dtype) for a in prepared),
        in_specs=[smem] + [pl.BlockSpec(memory_space=pltpu.HBM)] * 5,
        out_specs=(vmem,) * (2 + kinds),
        scratch_shapes=[pltpu.VMEM(a.shape, a.dtype) for a in raw]
        + [pltpu.SemaphoreType.DMA((5,))],
        compiler_params=pltpu.CompilerParams(vmem_limit_bytes=49152 * 1024),
    )(odd, *[pltpu.with_memory_space_constraint(a, pltpu.HBM) for a in raw])

    def moved(block, axes, pairs):
        return lax.ppermute(block, axes, pairs) if pairs else jnp.zeros_like(block)

    got_rims = [moved(rim, "gz", pairs_of("gz", n)) for n, rim in enumerate(rims)]
    got_planes = [moved(plane, "gy", pairs_of("gy", n)) for n, plane in enumerate((even, other))]

    def facing(row, rim):
        return jnp.concatenate([row] + [rim[n, :, xs : xs + xs // 2] for n in range(2)], 1)

    low, high = ([facing(rim[y, :, :xs], rim) for rim in got_rims] for y in (0, ys - 1))
    low, high = jnp.stack(low), jnp.stack(high)
    got_rows = [
        moved(jnp.where(odd_y == (n == 0), low, high), "gy", pairs_of("gy", n)) for n in range(2)
    ]

    first = jnp.transpose(kernel_first, (2, 3, 4, 1, 0)).reshape(27, c0, c1)
    second = jnp.transpose(kernel_second, (2, 3, 4, 1, 0)).reshape(27, c1, c2)
    sizes = (ys, zs, xs, c1, c2)
    wide = rows_of(27 * c1) * lanes
    up, places, side_up, side_places, cells, first, second, *orders = pl.pallas_call(
        functools.partial(side_kernel, sizes),
        out_shape=(
            like(ys, zs + 4, c2, lanes),
            like(ys, zs + 2, c1, lanes),
            like(2, 2, zs, c2, lanes),
            like(2, zs, c1, lanes),
            like(2 * ys, 4 * c0, 2 * zs * lanes),
            like(24, 9 * c1),
            like(3 * c1, 9 * c2),
            like(9, 4 * c0, lanes),
            like(9, 3 * c1, wide),
        ),
        in_specs=[smem, [vmem] * 2, [vmem] * kinds, [vmem] * 2, vmem, vmem, vmem],
        out_specs=(vmem,) * 9,
        compiler_params=params,
        cost_estimate=pl.CostEstimate(flops=10**7, bytes_accessed=10**6, transcendentals=0),
    )(odd, [even, other], got_rims, got_planes, volume, first, second)

    sizes1, sizes2 = 27 * c0 * c1 // dp, 27 * c1 * c2 // dp
    sum_rows = -(-(rows_of(sizes1) + rows_of(sizes2)) // 16) * 16
    grad_vol, sums = pl.pallas_call(
        functools.partial(main_kernel, sizes),
        out_shape=(like(*volume.shape[1:]), like(dp, sum_rows, lanes)),
        in_specs=[smem, [vmem] * 2, [vmem] * kinds, [vmem] * 2, [vmem] * 2] + [vmem] * 9,
        out_specs=(pl.BlockSpec(memory_space=pl.ANY), vmem),
        scratch_shapes=[
            pltpu.VMEM((2, 2, 4, c2, lanes), bf16),
            pltpu.VMEM((2 * ys + 4, 2 * zs + 4, c1, lanes), bf16),
            pltpu.VMEM(volume.shape[1:], f32),
            pltpu.VMEM(volume.shape[1:], bf16),
            pltpu.SemaphoreType.DMA((2 * ys,)),
        ],
        compiler_params=params,
        cost_estimate=pl.CostEstimate(
            flops=200_000_000, bytes_accessed=2_000_000, transcendentals=0
        ),
    )(
        odd,
        [even, other],
        got_rims,
        got_planes,
        got_rows,
        up,
        places,
        side_up,
        side_places,
        cells,
        first,
        second,
        *orders,
    )

    sent = jnp.broadcast_to(sums[:, None], (dp, gy * gz) + sums.shape[1:])
    sent = sent.reshape((dp * gy * gz,) + sums.shape[1:])
    got = lax.all_to_all(sent, ("dp", "gy", "gz"), 0, 0, tiled=True)
    count = volume.shape[0] * volume.shape[2] * volume.shape[3] * volume.shape[4] * dp * gy * gz
    total = jnp.sum(got.astype(f32), axis=0)
    split = rows_of(sizes2)
    second_out = total[:split].reshape(-1)[:sizes2] * math.sqrt(64.0 / count)
    first_out = total[split : split + rows_of(sizes1)].reshape(-1)[:sizes1]
    return grad_vol[None], first_out * math.sqrt(8.0 / count), second_out


def solution(mesh):
    cells = P("dp", None, "gy", "gz", None)
    return jax.shard_map(
        shards,
        mesh=mesh,
        in_specs=(cells,) * 6 + (P(), P()),
        out_specs=(cells, P("dp"), P("dp")),
        check_vma=False,
    )
```

profile of v0, /device:TPU:0, one launch (start us, length us, event | category | flops | bytes accessed | tf_op | source)
XLA Modules:
  0.0 35.0 jit_solution(8205853197591021408)
XLA Ops:
  0.6 0.1 add_convert_fusion.odd_ref
  0.7 0.0 copy-start.1
  0.7 0.0 copy-start.2
  0.7 1.8 %shard_map.103 = (bf16[6,32,128]{2,1,0:T(8,128)(2,1)S(1)}, bf16[6,32,128]{2,1,0:T(8,128)(2,1)S(1)}, bf16[2,32,128]{2,1,0:T(8,128)(2,1)S(1)}) custom-call(s32[2]{0:T(128)S(1)} %add_convert_fusion.odd_ref, bf16[1,32,1,4,32]{4,3,2,1,0:T(4,128)(2,1)} %refs_0_.1, bf16[1,32,1,4,32]{4,3,2,1,0:T(4,128)(2,1)} %refs_1_.1, s32[1,32,1,4,32]{4,3,2,1,0:T(4,128)} %refs_2_.1, ...), custom_call_target="tpu_custom_call" | custom-call | tf_op jit(solution)/shard_map/pallas_call | solution.py:438
  2.5 0.0 copy-start
  2.5 3.0 %collective-permute-start = (bf16[2,32,128]{2,1,0:T(8,128)(2,1)S(1)}, bf16[2,32,128]{2,1,0:T(8,128)(2,1)S(1)}, u32[]{:S(2)}, u32[]{:S(2)}) collective-permute-start(bf16[2,32,128]{2,1,0:T(8,128)(2,1)S(1)} %get-tuple-element.19), channel_id=1, source_target_pairs={{0,1},{1,0},{2,3},{3,2},{4,5},{5,4},{6,7},{7,6},{8,9},{9,8},{10,11... | collective-permute-start | bytes 49160 | tf_op jit(solution)/shard_map/ppermute | solution.py:449
  5.5 0.0 collective-permute-start.1
  5.5 0.7 %collective-permute-start.2 = (bf16[6,32,128]{2,1,0:T(8,128)(2,1)S(1)}, bf16[6,32,128]{2,1,0:T(8,128)(2,1)S(1)}, u32[]{:S(2)}, u32[]{:S(2)}) collective-permute-start(bf16[6,32,128]{2,1,0:T(8,128)(2,1)S(1)} %get-tuple-element.18.own_refs_1_), channel_id=1, source_target_pairs={{2,4},{4,2},{3,5},{5,3},{10,12},{12,10},{11,13},{13,11},{18,20},{2... | collective-permute-start | bytes 147464 | tf_op jit(solution)/shard_map/ppermute | solution.py:449
  6.2 1.0 %collective-permute-done.rim_refs_0_ = bf16[2,32,128]{2,1,0:T(8,128)(2,1)S(1)} collective-permute-done((bf16[2,32,128]{2,1,0:T(8,128)(2,1)S(1)}, bf16[2,32,128]{2,1,0:T(8,128)(2,1)S(1)}, u32[]{:S(2)}, u32[]{:S(2)}) %collective-permute-start) | collective-permute-done | bytes 16416 | tf_op jit(solution)/shard_map/ppermute | solution.py:449
  7.3 0.1 fusion.1
  7.3 0.1 broadcast_select_fusion
  7.4 0.7 %collective-permute-start.4 = (bf16[1,32,128]{2,1,0:T(8,128)(2,1)S(1)}, bf16[1,32,128]{2,1,0:T(8,128)(2,1)S(1)}, u32[]{:S(2)}, u32[]{:S(2)}) collective-permute-start(bf16[1,32,128]{2,1,0:T(8,128)(2,1)S(1)} %get-tuple-element.31), channel_id=1, source_target_pairs={{2,4},{4,2},{3,5},{5,3},{10,12},{12,10},{11,13},{13,11},{18,20},{2... | collective-permute-start | bytes 24584 | tf_op jit(solution)/shard_map/ppermute | solution.py:449
  8.1 3.8 %collective-permute-start.3 = (bf16[1,32,128]{2,1,0:T(8,128)(2,1)S(1)}, bf16[1,32,128]{2,1,0:T(8,128)(2,1)S(1)}, u32[]{:S(2)}, u32[]{:S(2)}) collective-permute-start(bf16[1,32,128]{2,1,0:T(8,128)(2,1)S(1)} %get-tuple-element.32), channel_id=1, source_target_pairs={{0,2},{4,6},{2,0},{6,4},{1,3},{5,7},{3,1},{7,5},{8,10},{12,14},{10... | collective-permute-start | bytes 24584 | tf_op jit(solution)/shard_map/ppermute | solution.py:449
  11.9 0.0 collective-permute-done.1.plane_refs_0_
  11.9 0.0 collective-permute-done.2.plane_refs_1_
  11.9 0.0 copy-done.1
  11.9 0.0 copy-done.2
  11.9 0.0 copy-done
  11.9 1.0 %shard_map.104 = (bf16[2,12,32,128]{3,2,1,0:T(8,128)(2,1)S(1)}, bf16[2,10,16,128]{3,2,1,0:T(8,128)(2,1)S(1)}, bf16[2,2,8,32,128]{4,3,2,1,0:T(8,128)(2,1)S(1)}, b...) custom-call(s32[2]{0:T(128)S(1)} %add_convert_fusion.odd_ref, ...), custom_call_target="tpu_custom_call" | custom-call | flops 10000000 | bytes 1000000 | tf_op jit(solution)/shard_map/pallas_call | solution.py:467
  12.9 0.0 collective-permute-done.4.row_refs_1_
  12.9 0.0 collective-permute-done.3.row_refs_0_
  12.9 4.4 %shard_map.105 = (bf16[4,4,16,128]{3,2,1,0:T(8,128)(2,1)}, bf16[4,32,128]{2,1,0:T(8,128)(2,1)S(1)}) custom-call(s32[2]{0:T(128)S(1)} %add_convert_fusion.odd_ref, bf16[6,32,128]{2,1,0:T(8,128)(2,1)S(1)} %get-tuple-element.17.own_refs_0_, bf16[6,32,128]{2,1,0:T(8,128)(2,1)S(1)} %get-tuple-element.18.own_refs_1_, ...), custom_call_target="tpu_custom_call" | custom-call | flops 200000000 | bytes 2000000 | tf_op jit(solution)/shard_map/pallas_call | solution.py:488
  17.4 16.3 %all_to_all.5 = bf16[32,32,128]{2,1,0:T(8,128)(2,1)S(1)} all-to-all(bf16[32,32,128]{2,1,0:T(8,128)(2,1)S(1)} %bitcast.16), channel_id=1, replica_groups=mesh['dp'=4,'gy'=4,'gz'=2] {'dp','gy','gz'}, dimensions={0} | all-to-all | bytes 524288 | tf_op jit(solution)/shard_map/all_to_all | solution.py:522
  33.8 0.6 %fusion = f32[3456]{0:T(1024)} fusion(f32[32,128]{1,0:T(8,128)S(1)} %convert_reduce_fusion), kind=kLoop, calls=%fused_computation.2 | loop fusion | flops 3456 | bytes 27648 | tf_op jit(solution)/shard_map/mul | solution.py:526
  34.4 0.6 %slice_multiply_fusion.1 = f32[432]{0:T(512)} fusion(f32[512]{0:T(512)S(1)} %slice_bitcast_fusion), kind=kLoop, calls=%fused_computation.8 | loop fusion | flops 432 | bytes 3456 | tf_op jit(solution)/shard_map/mul | solution.py:528
  (5 shorter events, 0.1 us)
Async XLA Ops:
  0.7 11.2 %copy-start.1 = (bf16[1,4,4,16,128]{4,3,2,1,0:T(8,128)(2,1)S(1)}, bf16[1,4,4,16,128]{4,3,2,1,0:T(8,128)(2,1)}, u32[]{:S(2)}) copy-start(bf16[1,4,4,16,128]{4,3,2,1,0:T(8,128)(2,1)} %volume_ref.1) | copy-start | bytes 196612
  0.7 11.2 %copy-start.2 = (bf16[16,4,3,3,3]{0,1,4,3,2:T(4,128)(2,1)S(1)}, bf16[16,4,3,3,3]{0,1,4,3,2:T(4,128)(2,1)}, u32[]{:S(2)}) copy-start(bf16[16,4,3,3,3]{0,1,4,3,2:T(4,128)(2,1)} %param.14) | copy-start | bytes 10372
  2.5 9.4 %copy-start = (bf16[32,16,3,3,3]{0,1,4,3,2:T(8,128)(2,1)S(1)}, bf16[32,16,3,3,3]{0,1,4,3,2:T(8,128)(2,1)}, u32[]{:S(2)}) copy-start(bf16[32,16,3,3,3]{0,1,4,3,2:T(8,128)(2,1)} %param.15) | copy-start | bytes 82948
  2.5 4.7 %collective-permute-start = (bf16[2,32,128]{2,1,0:T(8,128)(2,1)S(1)}, bf16[2,32,128]{2,1,0:T(8,128)(2,1)S(1)}, u32[]{:S(2)}, u32[]{:S(2)}) collective-permute-start(bf16[2,32,128]{2,1,0:T(8,128)(2,1)S(1)} %get-tuple-element.19), channel_id=1, source_target_pairs={{0,1},{1,0},{2,3},{3,2},{4,5},{5,4},{6,7},{7,6},{8,9},{9,8},{10,11... | collective-permute-start | bytes 49160 | tf_op jit(solution)/shard_map/ppermute | solution.py:449
  5.5 6.3 %collective-permute-start.1 = (bf16[6,32,128]{2,1,0:T(8,128)(2,1)S(1)}, bf16[6,32,128]{2,1,0:T(8,128)(2,1)S(1)}, u32[]{:S(2)}, u32[]{:S(2)}) collective-permute-start(bf16[6,32,128]{2,1,0:T(8,128)(2,1)S(1)} %get-tuple-element.17.own_refs_0_), channel_id=1, source_target_pairs={{0,2},{4,6},{2,0},{6,4},{1,3},{5,7},{3,1},{7,5},{8,10},{12,14},{10... | collective-permute-start | bytes 147464 | tf_op jit(solution)/shard_map/ppermute | solution.py:449
  5.5 6.3 %collective-permute-start.2 = (bf16[6,32,128]{2,1,0:T(8,128)(2,1)S(1)}, bf16[6,32,128]{2,1,0:T(8,128)(2,1)S(1)}, u32[]{:S(2)}, u32[]{:S(2)}) collective-permute-start(bf16[6,32,128]{2,1,0:T(8,128)(2,1)S(1)} %get-tuple-element.18.own_refs_1_), channel_id=1, source_target_pairs={{2,4},{4,2},{3,5},{5,3},{10,12},{12,10},{11,13},{13,11},{18,20},{2... | collective-permute-start | bytes 147464 | tf_op jit(solution)/shard_map/ppermute | solution.py:449
  7.4 5.5 %collective-permute-start.4 = (bf16[1,32,128]{2,1,0:T(8,128)(2,1)S(1)}, bf16[1,32,128]{2,1,0:T(8,128)(2,1)S(1)}, u32[]{:S(2)}, u32[]{:S(2)}) collective-permute-start(bf16[1,32,128]{2,1,0:T(8,128)(2,1)S(1)} %get-tuple-element.31), channel_id=1, source_target_pairs={{2,4},{4,2},{3,5},{5,3},{10,12},{12,10},{11,13},{13,11},{18,20},{2... | collective-permute-start | bytes 24584 | tf_op jit(solution)/shard_map/ppermute | solution.py:449
  8.1 4.8 %collective-permute-start.3 = (bf16[1,32,128]{2,1,0:T(8,128)(2,1)S(1)}, bf16[1,32,128]{2,1,0:T(8,128)(2,1)S(1)}, u32[]{:S(2)}, u32[]{:S(2)}) collective-permute-start(bf16[1,32,128]{2,1,0:T(8,128)(2,1)S(1)} %get-tuple-element.32), channel_id=1, source_target_pairs={{0,2},{4,6},{2,0},{6,4},{1,3},{5,7},{3,1},{7,5},{8,10},{12,14},{10... | collective-permute-start | bytes 24584 | tf_op jit(solution)/shard_map/ppermute | solution.py:449
where the time goes:
time: 35.1 us; the launch traced here: 35 us
  blocking collectives  16.3 us (46%)
  starting transfers between devices  8.1 us (23%)
  Pallas kernels  7.17 us (20%)
  other arithmetic  1.4 us (4%)
  waiting for transfers between devices  1.06 us (3%)
  between operations  0.76 us (2%)
    all_to_all x1, blocking collectives, shards(): got = lax.all_to_all(sent, ('dp', 'gy', 'gz'), 0, 0, tiled=True)  16.3 us
    ppermute x5, starting transfers between devices, moved(): return lax.ppermute(block, axes, pairs) if pairs else jnp.zeros_like(block)  8.1 us
    pallas_call x1, Pallas kernels, shards(): pl.pallas_call(functools.partial(main_kernel, sizes), out_shape=(like(*vo...  4.41 us
    pallas_call x1, Pallas kernels, shards(): pl.pallas_call(functools.partial(prepare_kernel, kinds), out_shape=tuple(...  1.78 us
    ppermute x5, waiting for transfers between devices, moved(): return lax.ppermute(block, axes, pairs) if pairs else jnp.zeros_like(block)  1.06 us
    pallas_call x1, Pallas kernels, shards(): pl.pallas_call(functools.partial(side_kernel, sizes), out_shape=(like(ys,...  0.98 us
  transfers between devices with their start and end apart: 5, of which 1 were waited for; matrix products, arithmetic and copies ran while one was open for 0% of the time, Pallas kernels for 3%

commit v1 on v0

--- a/solution.py
+++ b/solution.py
@@ -354,7 +354,7 @@
                         [pltpu.roll(act, 1, 1), act, pltpu.roll(act, lanes - 1, 1)], 0
                     ).astype(bf16)
                 )
-            term = dot_nt(jnp.concatenate(inputs, 1), around[:, lanes:-lanes])
+            term = dot_nt(around[:, lanes:-lanes], jnp.concatenate(inputs, 1))
             second_sum = term if second_sum is None else second_sum + term
 
     weights = first_ref[...]
@@ -382,10 +382,9 @@
         leaving_ref[:, y] = cells_ref[:, y].astype(bf16)
         leaving.append(pltpu.make_async_copy(leaving_ref.at[:, y], grad_ref.at[:, y], sent.at[y]))
         leaving[y].start()
-        term = dot_nt(volume_ref[y], around)
+        term = dot_nt(around, volume_ref[y])
         first_sum = term if first_sum is None else first_sum + term
 
-    first_sum, second_sum = first_sum.T, second_sum.T
     first, second = 0.0, 0.0
     for tap in range(9):
         first += dot(first_sum[tap * c1 : (tap + 1) * c1].astype(bf16), first_order_ref[tap])
@@ -484,7 +483,7 @@
     )(odd, [even, other], got_rims, got_planes, volume, first, second)
 
     sizes1, sizes2 = 27 * c0 * c1 // dp, 27 * c1 * c2 // dp
-    sum_rows = -(-(rows_of(sizes1) + rows_of(sizes2)) // 16) * 16
+    sum_rows = -(-(rows_of(sizes1) + rows_of(sizes2)) // 32) * 32
     grad_vol, sums = pl.pallas_call(
         functools.partial(main_kernel, sizes),
         out_shape=(like(*volume.shape[1:]), like(dp, sum_rows, lanes)),
@@ -517,11 +516,16 @@
         *orders,
     )
 
-    sent = jnp.broadcast_to(sums[:, None], (dp, gy * gz) + sums.shape[1:])
-    sent = sent.reshape((dp * gy * gz,) + sums.shape[1:])
+    half = sum_rows // 2
+    low, high = sums[:, :half], sums[:, half:]
+    other = lax.ppermute(jnp.where(odd_y, low, high), "gy", pairs_of("gy", 0))
+    part = jnp.where(odd_y, high, low).astype(f32) + other.astype(f32)
+    sent = jnp.broadcast_to(part.astype(bf16)[:, None], (dp, gy * gz) + part.shape[1:])
+    sent = sent.reshape((dp * gy * gz,) + part.shape[1:])
     got = lax.all_to_all(sent, ("dp", "gy", "gz"), 0, 0, tiled=True)
+    got = got.reshape((dp * gy // 2, 2, gz) + part.shape[1:])
     count = volume.shape[0] * volume.shape[2] * volume.shape[3] * volume.shape[4] * dp * gy * gz
-    total = jnp.sum(got.astype(f32), axis=0)
+    total = jnp.sum(got.astype(f32), axis=(0, 2)).reshape(sum_rows, lanes)
     split = rows_of(sizes2)
     second_out = total[:split].reshape(-1)[:sizes2] * math.sqrt(64.0 / count)
     first_out = total[split : split + rows_of(sizes1)].reshape(-1)[:sizes1]

time: 35.1 us -> 34.8 us (level)
  blocking collectives: 16.3 us -> 13.3 us
  starting transfers between devices: 8.1 us -> 9.48 us
  waiting for transfers between devices: 1.06 us -> 1.9 us
  Pallas kernels: 7.17 us -> 7.69 us
    all_to_all x1, blocking collectives: 16.3 us -> 13.3 us  [shards(): got = lax.all_to_all(sent, ('dp', 'gy', 'gz'), 0, 0, tiled=True)]
    ppermute x0 -> x1, starting transfers between devices: none -> 1.39 us  [shards(): other = lax.ppermute(jnp.where(odd_y, low, high), 'gy', pairs_of('gy', 0))]
    ppermute x0 -> x1, waiting for transfers between devices: none -> 0.84 us  [shards(): other = lax.ppermute(jnp.where(odd_y, low, high), 'gy', pairs_of('gy', 0))]
    pallas_call x1, Pallas kernels: 4.41 us -> 4.93 us  [shards(): pl.pallas_call(functools.partial(main_kernel, sizes), out_shape=(like(*vo...]
  transfers between devices with their start and end apart: 5 -> 6, of which waited for: 1 -> 2; matrix products, arithmetic and copies ran while one was open for 0% -> 0% of each run, Pallas kernels for 3% -> 3%
where the time goes in v1:
time: 34.8 us; the launch traced here: 34.7 us
  blocking collectives  13.3 us (38%)
  starting transfers between devices  9.48 us (27%)
  Pallas kernels  7.69 us (22%)
  waiting for transfers between devices  1.9 us (5%)
  other arithmetic  1.39 us (4%)
  between operations  0.77 us (2%)
    all_to_all x1, blocking collectives, shards(): got = lax.all_to_all(sent, ('dp', 'gy', 'gz'), 0, 0, tiled=True)  13.3 us
    ppermute x5, starting transfers between devices, moved(): return lax.ppermute(block, axes, pairs) if pairs else jnp.zeros_like(block)  8.1 us
    pallas_call x1, Pallas kernels, shards(): pl.pallas_call(functools.partial(main_kernel, sizes), out_shape=(like(*vo...  4.93 us
    pallas_call x1, Pallas kernels, shards(): pl.pallas_call(functools.partial(prepare_kernel, kinds), out_shape=tuple(...  1.78 us
    ppermute x1, starting transfers between devices, shards(): other = lax.ppermute(jnp.where(odd_y, low, high), 'gy', pairs_of('gy', 0))  1.39 us
    ppermute x5, waiting for transfers between devices, moved(): return lax.ppermute(block, axes, pairs) if pairs else jnp.zeros_like(block)  1.06 us
    pallas_call x1, Pallas kernels, shards(): pl.pallas_call(functools.partial(side_kernel, sizes), out_shape=(like(ys,...  0.98 us
    ppermute x1, waiting for transfers between devices, shards(): other = lax.ppermute(jnp.where(odd_y, low, high), 'gy', pairs_of('gy', 0))  0.84 us
  transfers between devices with their start and end apart: 6, of which 2 were waited for; matrix products, arithmetic and copies ran while one was open for 0% of the time, Pallas kernels for 3%

profile of v1, /device:TPU:0, one launch (start us, length us, event | category | flops | bytes accessed | tf_op | source)
XLA Modules:
  0.0 34.7 jit_solution(5971562726644957372)
XLA Ops:
  0.6 0.1 add_convert_fusion.1.odd_ref
  0.7 0.0 copy-start.1
  0.7 0.0 copy-start.2
  0.7 1.8 %shard_map.103 = (bf16[6,32,128]{2,1,0:T(8,128)(2,1)S(1)}, bf16[6,32,128]{2,1,0:T(8,128)(2,1)S(1)}, bf16[2,32,128]{2,1,0:T(8,128)(2,1)S(1)}) custom-call(s32[2]{0:T(128)S(1)} %add_convert_fusion.1.odd_ref, bf16[1,32,1,4,32]{4,3,2,1,0:T(4,128)(2,1)} %refs_0_.1, bf16[1,32,1,4,32]{4,3,2,1,0:T(4,128)(2,1)} %refs_1_.1, s32[1,32,1,4,32]{4,3,2,1,0:T(4,128)} %refs_2_.1, ...), custom_call_target="tpu_custom_call" | custom-call | tf_op jit(solution)/shard_map/pallas_call | solution.py:437
  2.5 0.0 copy-start
  2.5 3.0 %collective-permute-start = (bf16[2,32,128]{2,1,0:T(8,128)(2,1)S(1)}, bf16[2,32,128]{2,1,0:T(8,128)(2,1)S(1)}, u32[]{:S(2)}, u32[]{:S(2)}) collective-permute-start(bf16[2,32,128]{2,1,0:T(8,128)(2,1)S(1)} %get-tuple-element.19), channel_id=1, source_target_pairs={{0,1},{1,0},{2,3},{3,2},{4,5},{5,4},{6,7},{7,6},{8,9},{9,8},{10,11... | collective-permute-start | bytes 49160 | tf_op jit(solution)/shard_map/ppermute | solution.py:448
  5.5 0.0 collective-permute-start.1
  5.5 0.7 %collective-permute-start.2 = (bf16[6,32,128]{2,1,0:T(8,128)(2,1)S(1)}, bf16[6,32,128]{2,1,0:T(8,128)(2,1)S(1)}, u32[]{:S(2)}, u32[]{:S(2)}) collective-permute-start(bf16[6,32,128]{2,1,0:T(8,128)(2,1)S(1)} %get-tuple-element.18.own_refs_1_), channel_id=1, source_target_pairs={{2,4},{4,2},{3,5},{5,3},{10,12},{12,10},{11,13},{13,11},{18,20},{2... | collective-permute-start | bytes 147464 | tf_op jit(solution)/shard_map/ppermute | solution.py:448
  6.2 1.0 %collective-permute-done.rim_refs_0_ = bf16[2,32,128]{2,1,0:T(8,128)(2,1)S(1)} collective-permute-done((bf16[2,32,128]{2,1,0:T(8,128)(2,1)S(1)}, bf16[2,32,128]{2,1,0:T(8,128)(2,1)S(1)}, u32[]{:S(2)}, u32[]{:S(2)}) %collective-permute-start) | collective-permute-done | bytes 16416 | tf_op jit(solution)/shard_map/ppermute | solution.py:448
  7.3 0.1 fusion.1
  7.3 0.1 broadcast_select_fusion.1
  7.4 0.7 %collective-permute-start.4 = (bf16[1,32,128]{2,1,0:T(8,128)(2,1)S(1)}, bf16[1,32,128]{2,1,0:T(8,128)(2,1)S(1)}, u32[]{:S(2)}, u32[]{:S(2)}) collective-permute-start(bf16[1,32,128]{2,1,0:T(8,128)(2,1)S(1)} %get-tuple-element.31), channel_id=1, source_target_pairs={{2,4},{4,2},{3,5},{5,3},{10,12},{12,10},{11,13},{13,11},{18,20},{2... | collective-permute-start | bytes 24584 | tf_op jit(solution)/shard_map/ppermute | solution.py:448
  8.1 3.8 %collective-permute-start.3 = (bf16[1,32,128]{2,1,0:T(8,128)(2,1)S(1)}, bf16[1,32,128]{2,1,0:T(8,128)(2,1)S(1)}, u32[]{:S(2)}, u32[]{:S(2)}) collective-permute-start(bf16[1,32,128]{2,1,0:T(8,128)(2,1)S(1)} %get-tuple-element.32), channel_id=1, source_target_pairs={{0,2},{4,6},{2,0},{6,4},{1,3},{5,7},{3,1},{7,5},{8,10},{12,14},{10... | collective-permute-start | bytes 24584 | tf_op jit(solution)/shard_map/ppermute | solution.py:448
  11.9 0.0 collective-permute-done.1.plane_refs_0_
  11.9 0.0 collective-permute-done.2.plane_refs_1_
  11.9 0.0 copy-done.1
  11.9 0.0 copy-done.2
  11.9 0.0 copy-done
  11.9 1.0 %shard_map.104 = (bf16[2,12,32,128]{3,2,1,0:T(8,128)(2,1)S(1)}, bf16[2,10,16,128]{3,2,1,0:T(8,128)(2,1)S(1)}, bf16[2,2,8,32,128]{4,3,2,1,0:T(8,128)(2,1)S(1)}, b...) custom-call(s32[2]{0:T(128)S(1)} %add_convert_fusion.1.odd_ref, ...), custom_call_target="tpu_custom_call" | custom-call | flops 10000000 | bytes 1000000 | tf_op jit(solution)/shard_map/pallas_call | solution.py:466
  12.9 0.0 collective-permute-done.4.row_refs_1_
  12.9 0.0 collective-permute-done.3.row_refs_0_
  12.9 4.9 %shard_map.105 = (bf16[4,4,16,128]{3,2,1,0:T(8,128)(2,1)}, bf16[4,32,128]{2,1,0:T(8,128)(2,1)S(1)}) custom-call(s32[2]{0:T(128)S(1)} %add_convert_fusion.1.odd_ref, bf16[6,32,128]{2,1,0:T(8,128)(2,1)S(1)} %get-tuple-element.17.own_refs_0_, bf16[6,32,128]{2,1,0:T(8,128)(2,1)S(1)} %get-tuple-element.18.own_refs_1_, ...), custom_call_target="tpu_custom_call" | custom-call | flops 200000000 | bytes 2000000 | tf_op jit(solution)/shard_map/pallas_call | solution.py:487
  17.9 1.4 %collective-permute-start.5 = (bf16[4,16,128]{2,1,0:T(8,128)(2,1)S(1)}, bf16[4,16,128]{2,1,0:T(8,128)(2,1)S(1)}, u32[]{:S(2)}, u32[]{:S(2)}) collective-permute-start(bf16[4,16,128]{2,1,0:T(8,128)(2,1)S(1)} %broadcast_select_fusion), channel_id=1, source_target_pairs={{0,2},{4,6},{2,0},{6,4},{1,3},{5,7},{3,1},{7,5},{8,10},{12,14},{10... | collective-permute-start | bytes 49160 | tf_op jit(solution)/shard_map/ppermute | solution.py:521
  19.2 0.8 %collective-permute-done.5 = bf16[4,16,128]{2,1,0:T(8,128)(2,1)S(1)} collective-permute-done((bf16[4,16,128]{2,1,0:T(8,128)(2,1)S(1)}, bf16[4,16,128]{2,1,0:T(8,128)(2,1)S(1)}, u32[]{:S(2)}, u32[]{:S(2)}) %collective-permute-start.5) | collective-permute-done | bytes 16416 | tf_op jit(solution)/shard_map/ppermute | solution.py:521
  20.1 13.3 %all_to_all.5 = bf16[32,16,128]{2,1,0:T(8,128)(2,1)S(1)} all-to-all(bf16[32,16,128]{2,1,0:T(8,128)(2,1)S(1)} %bitcast.19), channel_id=1, replica_groups=mesh['dp'=4,'gy'=4,'gz'=2] {'dp','gy','gz'}, dimensions={0} | all-to-all | bytes 262144 | tf_op jit(solution)/shard_map/all_to_all | solution.py:525
  33.5 0.6 %fusion = f32[3456]{0:T(1024)} fusion(f32[32,128]{1,0:T(8,128)S(1)} %bitcast.22), kind=kLoop, calls=%fused_computation.3 | loop fusion | flops 3456 | bytes 27648 | tf_op jit(solution)/shard_map/mul | solution.py:530
  34.1 0.6 %slice_multiply_fusion.1 = f32[432]{0:T(512)} fusion(f32[512]{0:T(512)S(1)} %slice_bitcast_fusion), kind=kLoop, calls=%fused_computation.10 | loop fusion | flops 432 | bytes 3456 | tf_op jit(solution)/shard_map/mul | solution.py:532
  (7 shorter events, 0.1 us)
Async XLA Ops:
  0.7 11.2 %copy-start.1 = (bf16[1,4,4,16,128]{4,3,2,1,0:T(8,128)(2,1)S(1)}, bf16[1,4,4,16,128]{4,3,2,1,0:T(8,128)(2,1)}, u32[]{:S(2)}) copy-start(bf16[1,4,4,16,128]{4,3,2,1,0:T(8,128)(2,1)} %volume_ref.1) | copy-start | bytes 196612
  0.7 11.2 %copy-start.2 = (bf16[16,4,3,3,3]{0,1,4,3,2:T(4,128)(2,1)S(1)}, bf16[16,4,3,3,3]{0,1,4,3,2:T(4,128)(2,1)}, u32[]{:S(2)}) copy-start(bf16[16,4,3,3,3]{0,1,4,3,2:T(4,128)(2,1)} %param.14) | copy-start | bytes 10372
  2.5 9.4 %copy-start = (bf16[32,16,3,3,3]{0,1,4,3,2:T(8,128)(2,1)S(1)}, bf16[32,16,3,3,3]{0,1,4,3,2:T(8,128)(2,1)}, u32[]{:S(2)}) copy-start(bf16[32,16,3,3,3]{0,1,4,3,2:T(8,128)(2,1)} %param.15) | copy-start | bytes 82948
  2.5 4.7 %collective-permute-start = (bf16[2,32,128]{2,1,0:T(8,128)(2,1)S(1)}, bf16[2,32,128]{2,1,0:T(8,128)(2,1)S(1)}, u32[]{:S(2)}, u32[]{:S(2)}) collective-permute-start(bf16[2,32,128]{2,1,0:T(8,128)(2,1)S(1)} %get-tuple-element.19), channel_id=1, source_target_pairs={{0,1},{1,0},{2,3},{3,2},{4,5},{5,4},{6,7},{7,6},{8,9},{9,8},{10,11... | collective-permute-start | bytes 49160 | tf_op jit(solution)/shard_map/ppermute | solution.py:448
  5.5 6.3 %collective-permute-start.1 = (bf16[6,32,128]{2,1,0:T(8,128)(2,1)S(1)}, bf16[6,32,128]{2,1,0:T(8,128)(2,1)S(1)}, u32[]{:S(2)}, u32[]{:S(2)}) collective-permute-start(bf16[6,32,128]{2,1,0:T(8,128)(2,1)S(1)} %get-tuple-element.17.own_refs_0_), channel_id=1, source_target_pairs={{0,2},{4,6},{2,0},{6,4},{1,3},{5,7},{3,1},{7,5},{8,10},{12,14},{10... | collective-permute-start | bytes 147464 | tf_op jit(solution)/shard_map/ppermute | solution.py:448
  5.5 6.3 %collective-permute-start.2 = (bf16[6,32,128]{2,1,0:T(8,128)(2,1)S(1)}, bf16[6,32,128]{2,1,0:T(8,128)(2,1)S(1)}, u32[]{:S(2)}, u32[]{:S(2)}) collective-permute-start(bf16[6,32,128]{2,1,0:T(8,128)(2,1)S(1)} %get-tuple-element.18.own_refs_1_), channel_id=1, source_target_pairs={{2,4},{4,2},{3,5},{5,3},{10,12},{12,10},{11,13},{13,11},{18,20},{2... | collective-permute-start | bytes 147464 | tf_op jit(solution)/shard_map/ppermute | solution.py:448
  7.4 5.5 %collective-permute-start.4 = (bf16[1,32,128]{2,1,0:T(8,128)(2,1)S(1)}, bf16[1,32,128]{2,1,0:T(8,128)(2,1)S(1)}, u32[]{:S(2)}, u32[]{:S(2)}) collective-permute-start(bf16[1,32,128]{2,1,0:T(8,128)(2,1)S(1)} %get-tuple-element.31), channel_id=1, source_target_pairs={{2,4},{4,2},{3,5},{5,3},{10,12},{12,10},{11,13},{13,11},{18,20},{2... | collective-permute-start | bytes 24584 | tf_op jit(solution)/shard_map/ppermute | solution.py:448
  8.1 4.8 %collective-permute-start.3 = (bf16[1,32,128]{2,1,0:T(8,128)(2,1)S(1)}, bf16[1,32,128]{2,1,0:T(8,128)(2,1)S(1)}, u32[]{:S(2)}, u32[]{:S(2)}) collective-permute-start(bf16[1,32,128]{2,1,0:T(8,128)(2,1)S(1)} %get-tuple-element.32), channel_id=1, source_target_pairs={{0,2},{4,6},{2,0},{6,4},{1,3},{5,7},{3,1},{7,5},{8,10},{12,14},{10... | collective-permute-start | bytes 24584 | tf_op jit(solution)/shard_map/ppermute | solution.py:448
  17.9 2.2 %collective-permute-start.5 = (bf16[4,16,128]{2,1,0:T(8,128)(2,1)S(1)}, bf16[4,16,128]{2,1,0:T(8,128)(2,1)S(1)}, u32[]{:S(2)}, u32[]{:S(2)}) collective-permute-start(bf16[4,16,128]{2,1,0:T(8,128)(2,1)S(1)} %broadcast_select_fusion), channel_id=1, source_target_pairs={{0,2},{4,6},{2,0},{6,4},{1,3},{5,7},{3,1},{7,5},{8,10},{12,14},{10... | collective-permute-start | bytes 49160 | tf_op jit(solution)/shard_map/ppermute | solution.py:521
